TPU v7x, 512 devices: a whole 4x4x16 slice. The times are simulated.
512 devices in a mesh: dp: 64 (over z, x), tensor: 8 (over y, core).
Axes of the slice: x: 4, y: 4, z: 16, core: 2. Of those that a mesh axis runs over, the one named last changes fastest.
Arguments:
- queries: bfloat16 [16384, 5120], P('dp', 'tensor'), may hold values from -6 to 6
- branch_keys: bfloat16 [16384, 1024], P('dp', 'tensor'), may hold values from -6 to 6
- branch_values: bfloat16 [16384, 1024], P('dp', 'tensor'), may hold values from -6 to 6
- shared_keys: bfloat16 [4096, 1024], P('dp', 'tensor'), may hold values from -6 to 6
- shared_values: bfloat16 [4096, 1024], P('dp', 'tensor'), may hold values from -6 to 6
- ancestry: int32 [64, 64], replicated, may hold values from 0 to 1, as said below
- plan: int32 [2048], replicated, may hold values from 0 to 63, as said below
Outputs:
- attended: bfloat16 [2048, 8, 5120], P('dp', 'tensor')
Inputs may be any that keep to these rules, and one draw needn't show every extreme that they name: ancestry[b, s] is 1 where shared block s is an ancestor of branch b. Every branch has 6 or more and at most 12 ancestor blocks; in every draw some branch has exactly 12. Unit u = 32 * d + j lies on index d of dp and goes to plan[u]. For each j the units j of all indices go to different indices, so every index receives exactly one unit j. Each index sends to 32 indices exactly 1 units each.
All inputs are finite; a program needn't handle non-finite values.
Results may differ from a plain program's by a relative error of at most 0.015.
Values may be sent and summed in bfloat16 or wider, within the bound.
A program may use at most 128 MiB of HBM per device.

v0:
```python
import math

import jax
import jax.numpy as jnp
from jax import lax
from jax.sharding import PartitionSpec as P

HEADS = 40
KV_HEADS = 8
HEAD_DIM = 128
STEP = 256
BLOCK = 64
UNIT = 8


negative_fill = -1e30


def spread_heads(values):
    return jnp.repeat(values, HEAD_DIM, axis=1)


def combine_parts(local_out, local_max, local_sum, shared_stats):
    shared_max, shared_sum, shared_acc = shared_stats
    top_value = jnp.maximum(local_max, shared_max)
    first_weight = local_sum * jnp.exp(local_max - top_value)
    second_weight = jnp.exp(shared_max - top_value)
    numerator = (
        spread_heads(first_weight) * local_out.astype(jnp.float32)
        + spread_heads(second_weight) * shared_acc
    )
    return (numerator / spread_heads(first_weight + second_weight * shared_sum)).astype(
        jnp.bfloat16
    )


def attend_shared(query_rows, ancestor_rows, shared_keys, shared_values, groups, per_group):
    row_count = query_rows.shape[0]
    width_here = query_rows.shape[1]
    heads_here = groups * per_group
    scale_factor = 1.0 / math.sqrt(HEAD_DIM)
    query_grid = query_rows.reshape(row_count, groups, per_group, HEAD_DIM)
    piece_keys = lax.all_gather(shared_keys, "dp", axis=0, tiled=True)
    piece_values = lax.all_gather(shared_values, "dp", axis=0, tiled=True)
    piece_rows = piece_keys.shape[0]
    block_ids = jnp.arange(piece_rows, dtype=jnp.int32) // BLOCK
    allowed = jnp.take(ancestor_rows, block_ids, axis=1) > 0
    running_max = jnp.full((row_count, heads_here), negative_fill, jnp.float32)
    running_acc = jnp.zeros((row_count, width_here), jnp.float32)
    key_grid = piece_keys.reshape(piece_rows, groups, HEAD_DIM)
    value_grid = piece_values.reshape(piece_rows, groups, HEAD_DIM)
    scores = (
        jnp.einsum("rghd,pgd->ghpr", query_grid, key_grid, preferred_element_type=jnp.float32)
        * scale_factor
    )
    visible = jnp.transpose(allowed)[None, None]
    scores = jnp.where(visible, scores, negative_fill)
    piece_max = jnp.transpose(jnp.max(scores, axis=2), (2, 0, 1)).reshape(row_count, heads_here)
    new_max = jnp.maximum(running_max, piece_max)
    column_max = jnp.transpose(new_max.reshape(row_count, groups, per_group), (1, 2, 0))[
        :, :, None, :
    ]
    weights = jnp.where(visible, jnp.exp(scores - column_max), 0.0)
    rescale = jnp.exp(running_max - new_max)
    piece_sum = jnp.transpose(jnp.sum(weights, axis=2), (2, 0, 1)).reshape(row_count, heads_here)
    product = jnp.einsum(
        "ghpr,pgd->rghd",
        weights.astype(jnp.bfloat16),
        value_grid,
        preferred_element_type=jnp.float32,
    ).reshape(row_count, width_here)
    return (new_max, piece_sum, running_acc * spread_heads(rescale) + product)


def body(queries, branch_keys, branch_values, shared_keys, shared_values, ancestry, plan):
    dp_count = lax.axis_size("dp")
    dp_index = lax.axis_index("dp")
    row_count = queries.shape[0]
    width_here = queries.shape[1]
    groups = branch_keys.shape[1] // HEAD_DIM
    per_group = HEADS // KV_HEADS
    heads_here = groups * per_group
    units_dev = row_count // UNIT
    capacity = max(1, 2 * units_dev // dp_count)
    branch_count = row_count // STEP
    scale_factor = 1.0 / math.sqrt(HEAD_DIM)
    query_grid = queries.reshape(branch_count, STEP, groups, per_group, HEAD_DIM)
    key_grid = branch_keys.reshape(branch_count, STEP, groups, HEAD_DIM)
    value_grid = branch_values.reshape(branch_count, STEP, groups, HEAD_DIM)
    causal_mask = jnp.arange(STEP)[:, None] >= jnp.arange(STEP)[None, :]
    local_scores = (
        jnp.einsum("bpghd,bqgd->bghpq", query_grid, key_grid, preferred_element_type=jnp.float32)
        * scale_factor
    )
    local_scores = jnp.where(causal_mask, local_scores, negative_fill)
    max_grid = jnp.max(local_scores, axis=-1)
    local_exp = jnp.where(causal_mask, jnp.exp(local_scores - max_grid[..., None]), 0.0)
    sum_grid = jnp.sum(local_exp, axis=-1)
    local_prod = jnp.einsum(
        "bghpq,bqgd->bpghd",
        local_exp.astype(jnp.bfloat16),
        value_grid,
        preferred_element_type=jnp.float32,
    )
    local_out = (
        (local_prod / jnp.transpose(sum_grid, (0, 3, 1, 2))[..., None])
        .reshape(row_count, width_here)
        .astype(jnp.bfloat16)
    )
    local_max = jnp.transpose(max_grid, (0, 3, 1, 2)).reshape(row_count, heads_here)
    local_sum = jnp.transpose(sum_grid, (0, 3, 1, 2)).reshape(row_count, heads_here)
    dest_table = plan.reshape(dp_count, units_dev)
    slot_ids = jnp.arange(units_dev, dtype=jnp.int32)
    my_dest = lax.dynamic_index_in_dim(dest_table, dp_index, 0, keepdims=False)
    buffer_slot = my_dest * capacity + slot_ids % capacity
    send_index = jnp.zeros((dp_count * capacity,), jnp.int32).at[buffer_slot].set(slot_ids)
    send_valid = jnp.zeros((dp_count * capacity,), jnp.bool_).at[buffer_slot].set(True)
    source_dev = jnp.sum(
        jnp.arange(dp_count, dtype=jnp.int32)[:, None] * (dest_table == dp_index).astype(jnp.int32),
        axis=0,
    )
    pick_index = source_dev * capacity + slot_ids % capacity
    first_branch = dp_index * branch_count
    ancestor_rows = jnp.repeat(
        lax.dynamic_slice_in_dim(ancestry, first_branch, branch_count, 0), STEP, axis=0
    )
    shared_stats = attend_shared(
        queries, ancestor_rows, shared_keys, shared_values, groups, per_group
    )
    merged = combine_parts(local_out, local_max, local_sum, shared_stats)
    unit_array = merged.reshape(units_dev, UNIT, width_here)
    taken = jnp.take(unit_array, send_index, axis=0)
    mask_shape = (dp_count * capacity,) + (1,) * (unit_array.ndim - 1)
    kept = jnp.where(send_valid.reshape(mask_shape), taken, jnp.zeros_like(taken))
    moved = lax.all_to_all(
        lax.all_to_all(
            kept.reshape((dp_count, capacity) + unit_array.shape[1:]),
            "dp",
            split_axis=0,
            concat_axis=0,
            tiled=True,
        ),
        "tensor",
        split_axis=2,
        concat_axis=3,
        tiled=True,
    )
    flat = moved.reshape((dp_count * capacity,) + moved.shape[2:])
    return jnp.take(flat, pick_index, axis=0)


def solution(mesh):
    return jax.shard_map(
        body,
        mesh=mesh,
        in_specs=(
            P("dp", "tensor"),
            P("dp", "tensor"),
            P("dp", "tensor"),
            P("dp", "tensor"),
            P("dp", "tensor"),
            P(),
            P(),
        ),
        out_specs=P("dp", "tensor", None),
        check_vma=False,
    )
```

profile of v0, /device:TPU:1, one launch (start us, length us, event | category | flops | bytes accessed | tf_op | source)
XLA Modules:
  0.0 374.7 jit_solution(11470409277885699871)
XLA Ops:
  6.5 0.7 all-gather.3.cloned.1.call-update
  7.3 0.7 all-gather.5.cloned.1.call-update
  8.1 0.8 reshape.244
  8.8 0.7 scatter_custom_fusion.1
  9.6 0.7 dynamic-slice_bitcast_fusion
  10.3 1.1 copy.27
  11.5 0.4 fusion.55
  12.1 1.3 fusion.21
  13.4 0.4 copy.32
  14.0 0.9 scatter_custom_fusion
  15.0 16.1 %gather_fusion = s32[4096,256]{1,0:T(8,128)} fusion(s32[256,64]{0,1:T(8,128)S(1)} %reshape.248, s32[4096]{0:T(1024)S(1)} %broadcast_clamp_fusion), kind=kCustom, calls=%fused_computation | custom fusion | bytes 8404992 | tf_op jit(solution)/shard_map/jit(_take)/gather | solution.py:47
  31.0 2.7 select_compare_fusion
  33.8 111.3 %all-gather.3.cloned.1.call-done = bf16[4096,128]{1,0:T(8,128)(2,1)} async-done(((bf16[64,128]{1,0:T(8,128)(2,1)}), bf16[4096,128]{1,0:T(8,128)(2,1)}) %all-gather.3.cloned.1.call-update) | async-done | bytes 1048592 | tf_op jit(solution)/shard_map/all_gather | solution.py:43
  145.1 4.6 %bitcast_reduce_fusion = (f32[5,256]{1,0:T(8,128)S(1)}, f32[4096,256,5]{1,0,2:T(8,128)S(1)}) fusion(pred[4096,256]{1,0:T(8,128)(4,1)S(1)} %select_compare_fusion, bf16[256,5,128]{0,2,1:T(8,128)(2,1)S(1)} %bitcast.155, bf16[4096,128]{1,0:T(8,128)(2,1)} %all-gather.3.cloned.1.call-done), kind=kOutput, calls=%fused_computation.6 | convolution fusion | flops 1357904640 | bytes 23401472 | tf_op jit(solution)/shard_map/rghd,pgd->ghpr/dot_general | solution.py:53
  149.7 5.2 %fusion.2 = f32[5,256]{1,0:T(8,128)S(1)} fusion(f32[4096,256,5]{1,0,2:T(8,128)S(1)} %get-tuple-element.10, f32[5,256]{1,0:T(8,128)S(1)} %broadcast_maximum_fusion, pred[4096,256]{1,0:T(8,128)(4,1)S(1)} %select_compare_fusion), kind=kLoop, calls=%fused_computation.10 | loop fusion | flops 26213120 | bytes 22030336 | tf_op jit(solution)/shard_map/reduce_sum | solution.py:65
  154.9 1.7 copy-done.1
  157.1 0.8 copy.34
  157.9 125.2 %all-gather.5.cloned.1.call-done = bf16[4096,128]{1,0:T(8,128)(2,1)} async-done(((bf16[64,128]{1,0:T(8,128)(2,1)}), bf16[4096,128]{1,0:T(8,128)(2,1)}) %all-gather.5.cloned.1.call-update) | async-done | bytes 1048592 | tf_op jit(solution)/shard_map/all_gather | solution.py:44
  283.1 10.2 %fusion.11 = f32[256,1,5,128]{3,0,2,1:T(8,128)S(1)} fusion(f32[4096,256,5]{1,0,2:T(8,128)} %copy-done.1, f32[5,256]{1,0:T(8,128)S(1)} %broadcast_maximum_fusion, pred[4096,256]{1,0:T(8,128)(4,1)S(1)} %select_compare_fusion, bf16[4096,128]{1,0:T(8,128)(2,1)} %all-gather.5.cloned.1.call-done), kind=kOutput, calls=%fused_computation.22 | convolution fusion | flops 1368391680 | bytes 23729152 | tf_op jit(solution)/shard_map/ghpr,pgd->rghd/dot_general | solution.py:66
  293.3 0.4 copy.36
  293.9 1.2 broadcast_in_dim.134
  295.6 1.1 reshape.249
  297.0 1.0 reshape.251
  298.4 1.0 reshape.255
  299.4 1.7 divide_convert_fusion
  301.1 0.7 gather_fusion.1
  302.0 34.2 %all_to_all.14 = bf16[64,1,8,640]{3,2,1,0:T(8,128)(2,1)S(1)} all-to-all(bf16[64,1,8,640]{3,2,1,0:T(8,128)(2,1)S(1)} %fusion.25), channel_id=1, replica_groups=mesh['dp'=64,'tensor'=8] {'dp'}, dimensions={0} | all-to-all | bytes 1310720 | tf_op jit(solution)/shard_map/all_to_all | solution.py:136
  336.1 0.9 copy.39
  337.0 18.3 %all-to-all-start.1 = ((bf16[64,1,8,640]{3,0,1,2:T(8,128)(2,1)}), bf16[64,1,8,640]{3,0,1,2:T(8,128)(2,1)S(1)}, u32[]{:S(2)}, u32[]{:S(2)}) async-start(bf16[64,1,8,640]{3,0,1,2:T(8,128)(2,1)} %copy.39), calls=%async_computation.1 | async-start | bytes 1310720 | tf_op jit(solution)/shard_map/all_to_all | solution.py:135
  355.4 10.8 %all-to-all-done.1 = bf16[64,1,8,640]{3,0,1,2:T(8,128)(2,1)S(1)} async-done(((bf16[64,1,8,640]{3,0,1,2:T(8,128)(2,1)}), bf16[64,1,8,640]{3,0,1,2:T(8,128)(2,1)S(1)}, u32[]{:S(2)}, u32[]{:S(2)}) %all-to-all-start.1) | async-done | bytes 655392 | tf_op jit(solution)/shard_map/all_to_all | solution.py:135
  366.3 0.7 gather_fusion.2
  367.1 0.8 bitcast_select_fusion.2
  (34 shorter events, 2.7 us)
Async XLA Ops:
  6.5 4.9 %copy-start = (bf16[256,128]{1,0:T(8,128)(2,1)S(1)}, bf16[256,128]{1,0:T(8,128)(2,1)}, u32[]{:S(2)}) copy-start(bf16[256,128]{1,0:T(8,128)(2,1)} %param.8) | copy-start | bytes 196612
  6.5 138.5 %all-gather.3.cloned.1.call-start = ((), (), s32[]{:S(2)}) async-start(), calls=%async_computation.2 | async-start | bytes 1064960 | tf_op jit(solution)/shard_map/all_gather | solution.py:43
  7.3 275.8 %all-gather.5.cloned.1.call-start = ((), (), s32[]{:S(2)}) async-start(), calls=%async_computation.3 | async-start | bytes 1064960 | tf_op jit(solution)/shard_map/all_gather | solution.py:44
  149.7 7.0 %copy-start.1 = (f32[4096,256,5]{1,0,2:T(8,128)}, f32[4096,256,5]{1,0,2:T(8,128)S(1)}, u32[]{:S(2)}) copy-start(f32[4096,256,5]{1,0,2:T(8,128)S(1)} %get-tuple-element.10) | copy-start | bytes 62914564
  337.0 29.2 %all-to-all-start.1 = ((bf16[64,1,8,640]{3,0,1,2:T(8,128)(2,1)}), bf16[64,1,8,640]{3,0,1,2:T(8,128)(2,1)S(1)}, u32[]{:S(2)}, u32[]{:S(2)}) async-start(bf16[64,1,8,640]{3,0,1,2:T(8,128)(2,1)} %copy.39), calls=%async_computation.1 | async-start | bytes 1310720 | tf_op jit(solution)/shard_map/all_to_all | solution.py:135
Sparse Core Ops, SparseCore 0:
  10.3 134.7 all-gather.2
  148.0 134.9 all-gather.4
where the time goes:
time: 375 us
  waiting for transfers between devices  249 us (66%)
  blocking collectives  34.2 us (9%)
  local copies, waits for them, and re-layouts  32.3 us (9%)
  starting transfers between devices  18.4 us (5%)
  matrix products  16.5 us (4%)
  between operations  13.7 us (4%)
  other arithmetic  11.1 us (3%)
    all_gather x1, waiting for transfers between devices, attend_shared(): piece_values = lax.all_gather(shared_values, 'dp', axis=0, tiled=True)  125 us
    all_gather x1, waiting for transfers between devices, attend_shared(): piece_keys = lax.all_gather(shared_keys, 'dp', axis=0, tiled=True)  111 us
    all_to_all x1, blocking collectives, body(): lax.all_to_all(kept.reshape((dp_count, capacity) + unit_array.shape[1:]),...  34.2 us
    all_to_all x1, starting transfers between devices, body(): lax.all_to_all(lax.all_to_all(kept.reshape((dp_count, capacity) + unit_ar...  18.3 us
    gather x1, local copies, waits for them, and re-layouts, attend_shared(): allowed = jnp.take(ancestor_rows, block_ids, axis=1) > 0  16.1 us
    all_to_all x1, waiting for transfers between devices, body(): lax.all_to_all(lax.all_to_all(kept.reshape((dp_count, capacity) + unit_ar...  10.8 us
    dot_general x1, matrix products, attend_shared(): jnp.einsum('ghpr,pgd->rghd', weights.astype(jnp.bfloat16), value_grid, pr...  10.2 us
  transfers between devices with their start and end apart: 3, of which 3 were waited for; matrix products, arithmetic and copies ran while one was open for 10% of the time, Pallas kernels for 0%

commit v1 on v0

v1 whole, which is shorter than its diff:
```python
import math

import jax
import jax.numpy as jnp
from jax import lax
from jax.experimental import pallas as pl
from jax.experimental.pallas import tpu as pltpu
from jax.sharding import PartitionSpec as P

HEADS = 40
KV_HEADS = 8
HEAD_DIM = 128
STEP = 256
BLOCK = 64
UNIT = 8
UNITS_DEV = STEP // UNIT
SHARED = 64
MOST = 12
N_DP = 64
N_X = 4
N_Z = 16
N_T = 8
PER = HEADS // KV_HEADS
CHUNKS = (1, 2, 2)
N_CH = len(CHUNKS)
KEYS = STEP + MOST * BLOCK
SCALE = math.log2(math.e) / math.sqrt(HEAD_DIM)
FILL = -1e30
MESH = pl.DeviceIdType.MESH
BF = jnp.bfloat16
F32 = jnp.float32


def iota(shape, dim):
    return lax.broadcasted_iota(jnp.int32, shape, dim)


def dot(a, b, contract=((1,), (0,))):
    return lax.dot_general(a, b, (contract, ((), ())), preferred_element_type=F32)


def flag(mask):
    return jnp.where(mask, 1.0, 0.0).astype(BF)


def kernel(q, bk, bv, sk, sv, anc, plan, out, kbuf, vbuf, kcat, vcat, pack, pick, *rest):
    snd, rest = rest[:N_CH], rest[N_CH:]
    rcv, rest = rest[:N_CH], rest[N_CH:]
    tsnd, rest = rest[:N_CH], rest[N_CH:]
    trcv, rest = rest[:N_CH], rest[N_CH:]
    send_k, send_v, got_ka, got_va, got_kb, got_vc, got_kc, got_vb, a_send, a_got, t_send, t_got = rest

    dp = lax.axis_index("dp")
    t = lax.axis_index("tensor")
    z, x = lax.div(dp, N_X), lax.rem(dp, N_X)
    zm, zd = lax.rem(z, 4), lax.div(z, 4)

    def at(dz, dx):
        return lax.rem(z + (dz + N_Z), N_Z) * N_X + lax.rem(x + dx, N_X)

    far = [at(4 * i, 0) for i in (2, 1, 3)]
    near = [at(d, 0) for d in (1, -1, 2, -2)]
    side = [at(0, i) for i in (1, 2, 3)]

    barrier = pltpu.get_barrier_semaphore()
    for peer in far + near + side:
        pl.semaphore_signal(barrier, inc=1, device_id={"dp": peer}, device_id_type=MESH)
    for i in range(1, N_T):
        pl.semaphore_signal(
            barrier, inc=1, device_id={"tensor": lax.rem(t + i, N_T)}, device_id_type=MESH
        )
    pl.semaphore_wait(barrier, len(far) + len(near) + len(side) + N_T - 1)

    def put(src, dst, send, got, peer):
        pltpu.make_async_remote_copy(
            src_ref=src, dst_ref=dst, send_sem=send, recv_sem=got,
            device_id={"dp": peer}, device_id_type=MESH,
        ).start()

    def await_blocks(buf, count, sem):
        view = buf.at[pl.ds(0, count)]
        pltpu.make_async_copy(view, view, sem).wait()

    k_own = x * 16 + zm * 4 + zd
    v_own = zm * 16 + x * 4 + zd
    for peer in far:
        put(sk, kbuf.at[k_own], send_k, got_ka, peer)
    for peer in far:
        put(sv, vbuf.at[v_own], send_v, got_va, peer)
    kbuf[k_own] = sk[...]
    vbuf[v_own] = sv[...]

    def scan(s, carry):
        count, ids = carry
        hit = anc[dp, s] > 0
        ids = tuple(
            jnp.where(jnp.logical_and(hit, count == k), s, ids[k]) for k in range(MOST)
        )
        return count + jnp.where(hit, 1, 0), ids

    zero = jnp.int32(0)
    count, ids = lax.fori_loop(0, SHARED, scan, (zero, (zero,) * MOST))

    rows16 = flag(iota((N_DP, 16), 1) == (iota((N_DP, 16), 0) >> 2))
    spread = dot(rows16, plan[...].astype(F32).astype(BF))
    quarter = (iota((N_DP, 128), 1) >> 5) == (iota((N_DP, 128), 0) & 3)
    fold = flag((iota((128, UNITS_DEV), 0) & 31) == iota((128, UNITS_DEV), 1))
    table = dot(jnp.where(quarter, spread, 0.0).astype(BF), fold)
    widen = flag((iota((UNITS_DEV, STEP), 1) >> 3) == iota((UNITS_DEV, STEP), 0))
    dest = dot(table.astype(BF), widen)
    mine = jnp.sum(jnp.where(iota((N_DP, STEP), 0) == dp, dest, 0.0), axis=0, keepdims=True)
    row_code = mine.astype(jnp.int32) * UNIT + (iota((1, STEP), 1) & 7)
    pack[...] = flag(iota((N_DP * UNIT, STEP), 0) == row_code)
    to_me = flag(table == dp.astype(F32))
    by_row = flag((iota((STEP, UNITS_DEV), 0) & 31) == iota((STEP, UNITS_DEV), 1))
    source = dot(by_row, to_me, ((1,), (1,)))
    widen_dp = flag((iota((N_DP, N_DP * UNIT), 1) >> 3) == iota((N_DP, N_DP * UNIT), 0))
    source = dot(source.astype(BF), widen_dp)
    same_row = (iota((STEP, N_DP * UNIT), 0) >> 5) == (iota((STEP, N_DP * UNIT), 1) & 7)
    pick[...] = jnp.where(same_row, source, 0.0).astype(BF)

    def k_group(g):
        return kbuf.at[pl.ds(x * 16 + g * 4, 4)]

    def k_across(g):
        for peer in side:
            put(k_group(g), k_group(g), send_k, got_kc, peer)

    def to_near(buf, start, send, gots):
        whole = buf.at[pl.ds(start, 4)]
        put(whole, whole, send, gots[0], near[0])
        put(whole, whole, send, gots[1], near[1])
        put(buf.at[pl.ds(start, 2)], buf.at[pl.ds(start, 2)], send, gots[2], near[2])
        put(buf.at[pl.ds(start + 2, 2)], buf.at[pl.ds(start + 2, 2)], send, gots[2], near[3])

    await_blocks(kbuf, 3, got_ka)
    to_near(kbuf, x * 16 + zm * 4, send_k, [got_kb.at[0], got_kb.at[1], got_kb.at[2]])
    await_blocks(vbuf, 3, got_va)
    v_start = zm * 16 + x * 4
    for i in range(3):
        put(vbuf.at[pl.ds(v_start, 4)], vbuf.at[pl.ds(v_start, 4)], send_v, got_vc.at[i], side[i])
    k_across(zm)
    to_near(vbuf, v_start, send_v, [got_vb] * 3)
    kcat[pl.ds(0, STEP), :] = bk[...]
    vcat[pl.ds(0, STEP), :] = bv[...]
    for i, shift in enumerate((3, 1, 2)):
        await_blocks(kbuf, 4, got_kb.at[i])
        k_across(lax.rem(zm + shift, 4))
    for i in range(3):
        await_blocks(vbuf, 4, got_vc.at[i])
        to_near(vbuf, zm * 16 + lax.rem(x + 3 - i, 4) * 4, send_v, [got_vb] * 3)

    await_blocks(kbuf, 48, got_kc)
    for k in range(MOST):
        s = ids[k]
        bx, bz = s & 3, s >> 2
        kcat[pl.ds(STEP + k * BLOCK, BLOCK), :] = kbuf[bx * 16 + (bz & 3) * 4 + (bz >> 2)]
    await_blocks(vbuf, 48, got_vb)
    for k in range(MOST):
        s = ids[k]
        bx, bz = s & 3, s >> 2
        vcat[pl.ds(STEP + k * BLOCK, BLOCK), :] = vbuf[(bz & 3) * 16 + bx * 4 + (bz >> 2)]

    col = iota((1, KEYS), 1)
    bias = jnp.where(col < STEP + count * BLOCK, 0.0, FILL)
    causal = iota((STEP, STEP), 1) <= iota((STEP, STEP), 0)

    head = 0
    for c, heads in enumerate(CHUNKS):
        for h in range(heads):
            qh = q[:, pl.ds(head * HEAD_DIM, HEAD_DIM)]
            head += 1
            scores = dot(qh, kcat[...], ((1,), (1,)))
            local = jnp.where(causal, scores[:, :STEP], FILL)
            shared = scores[:, STEP:] + bias[:, STEP:]
            top = jnp.maximum(
                jnp.max(local, axis=1, keepdims=True), jnp.max(shared, axis=1, keepdims=True)
            )
            local = jnp.exp2((local - top) * SCALE)
            shared = jnp.exp2((shared - top) * SCALE)
            total = jnp.sum(local, axis=1, keepdims=True) + jnp.sum(shared, axis=1, keepdims=True)
            acc = dot(local.astype(BF), vcat[pl.ds(0, STEP), :]) + dot(
                shared.astype(BF), vcat[pl.ds(STEP, MOST * BLOCK), :]
            )
            merged = (acc / total).astype(BF)
            slots = dot(pack[...], merged).astype(BF)
            snd[c][:, :, pl.ds(h * HEAD_DIM, HEAD_DIM)] = slots.reshape(N_DP, UNIT, HEAD_DIM)

        def send_one(i, carry, c=c):
            peer = lax.rem(dp + i, N_DP)
            put(snd[c].at[peer], rcv[c].at[dp], a_send.at[c], a_got.at[c], peer)
            return carry

        lax.fori_loop(1, N_DP, send_one, 0)
        rcv[c][dp] = snd[c][dp]

    for c, heads in enumerate(CHUNKS):
        await_blocks(rcv[c], N_DP - 1, a_got.at[c])
        wide = heads * HEAD_DIM
        rows = dot(pick[...], rcv[c][...].reshape(N_DP * UNIT, wide)).astype(BF)
        tsnd[c][...] = rows.reshape(N_T, UNITS_DEV, wide)
        for i in range(1, N_T):
            peer = lax.rem(t + i, N_T)
            pltpu.make_async_remote_copy(
                src_ref=tsnd[c].at[peer], dst_ref=trcv[c].at[t],
                send_sem=t_send.at[c], recv_sem=t_got.at[c],
                device_id={"tensor": peer}, device_id_type=MESH,
            ).start()
        trcv[c][t] = tsnd[c][t]

    start = 0
    for c, heads in enumerate(CHUNKS):
        await_blocks(trcv[c], N_T - 1, t_got.at[c])
        wide = heads * HEAD_DIM
        for peer in range(N_T):
            out[:, pl.ds(peer * PER * HEAD_DIM + start, wide)] = trcv[c][peer]
        start += wide

    await_blocks(kbuf, 63, send_k)
    await_blocks(vbuf, 63, send_v)
    for c in range(N_CH):
        await_blocks(snd[c], N_DP - 1, a_send.at[c])
        await_blocks(tsnd[c], N_T - 1, t_send.at[c])


def body(queries, branch_keys, branch_values, shared_keys, shared_values, ancestry, plan):
    vmem = pl.BlockSpec(memory_space=pltpu.VMEM)
    smem = pl.BlockSpec(memory_space=pltpu.SMEM)
    widths = [heads * HEAD_DIM for heads in CHUNKS]
    dma = pltpu.SemaphoreType.DMA
    rows = pl.pallas_call(
        kernel,
        name="tree_step",
        out_shape=jax.ShapeDtypeStruct((UNITS_DEV, HEADS * HEAD_DIM), BF),
        in_specs=[vmem] * 5 + [smem, vmem],
        out_specs=vmem,
        scratch_shapes=[
            pltpu.VMEM((SHARED, BLOCK, HEAD_DIM), BF),
            pltpu.VMEM((SHARED, BLOCK, HEAD_DIM), BF),
            pltpu.VMEM((KEYS, HEAD_DIM), BF),
            pltpu.VMEM((KEYS, HEAD_DIM), BF),
            pltpu.VMEM((N_DP * UNIT, STEP), BF),
            pltpu.VMEM((STEP, N_DP * UNIT), BF),
            *[pltpu.VMEM((N_DP, UNIT, w), BF) for w in widths],
            *[pltpu.VMEM((N_DP, UNIT, w), BF) for w in widths],
            *[pltpu.VMEM((N_T, UNITS_DEV, w), BF) for w in widths],
            *[pltpu.VMEM((N_T, UNITS_DEV, w), BF) for w in widths],
            dma, dma, dma, dma, dma((3,)), dma((3,)), dma, dma,
            dma((N_CH,)), dma((N_CH,)), dma((N_CH,)), dma((N_CH,)),
        ],
        compiler_params=pltpu.CompilerParams(
            collective_id=0, has_side_effects=True, vmem_limit_bytes=40 << 20
        ),
    )(
        queries, branch_keys, branch_values, shared_keys, shared_values, ancestry,
        plan.reshape(16, 128),
    )
    return rows.reshape(UNITS_DEV, 1, HEADS * HEAD_DIM)


def solution(mesh):
    return jax.shard_map(
        body,
        mesh=mesh,
        in_specs=(
            P("dp", "tensor"),
            P("dp", "tensor"),
            P("dp", "tensor"),
            P("dp", "tensor"),
            P("dp", "tensor"),
            P(),
            P(),
        ),
        out_specs=P("dp", "tensor", None),
        check_vma=False,
    )
```

time: 375 us -> 89.3 us (0.24)
  waiting for transfers between devices: 249 us -> 0 us
  Pallas kernels: 0 us -> 82.6 us
  blocking collectives: 34.2 us -> 0 us
  local copies, waits for them, and re-layouts: 32.3 us -> 6.26 us
  starting transfers between devices: 18.4 us -> 0 us
  matrix products: 16.5 us -> 0 us
  between operations: 13.7 us -> 0.02 us
  other arithmetic: 11.1 us -> 0 us
    all_gather x2 -> x0, waiting for transfers between devices: 236 us -> none  [the longest x1 125 us: attend_shared(): piece_values = lax.all_gather(shared_values, 'dp', axis=0, tiled=True)]
    pallas_call x0 -> x1, Pallas kernels: none -> 82.6 us  [body(): pl.pallas_call(kernel, name='tree_step', out_shape=jax.ShapeDtypeStruct((...]
    all_to_all x1 -> x0, blocking collectives: 34.2 us -> none  [body(): lax.all_to_all(kept.reshape((dp_count, capacity) + unit_array.shape[1:]),...]
    all_to_all x1 -> x0, starting transfers between devices: 18.3 us -> none  [body(): lax.all_to_all(lax.all_to_all(kept.reshape((dp_count, capacity) + unit_ar...]
    gather x3 -> x0, local copies, waits for them, and re-layouts: 17.5 us -> none  [the longest x1 16.1 us: attend_shared(): allowed = jnp.take(ancestor_rows, block_ids, axis=1) > 0]
    dot_general x4 -> x0, matrix products: 16.5 us -> none  [the longest x1 10.2 us: attend_shared(): jnp.einsum('ghpr,pgd->rghd', weights.astype(jnp.bfloat16), value_grid, pr...]
    all_to_all x1 -> x0, waiting for transfers between devices: 10.8 us -> none  [body(): lax.all_to_all(lax.all_to_all(kept.reshape((dp_count, capacity) + unit_ar...]
    reduce_sum x3 -> x0, other arithmetic: 5.52 us -> none  [the longest x1 5.25 us: attend_shared(): jnp.sum(weights, axis=2)]
  transfers between devices with their start and end apart: 3 -> 0, of which waited for: 3 -> 0; matrix products, arithmetic and copies ran while one was open for 10% -> 0% of each run, Pallas kernels for 0% -> 0%
where the time goes in v1:
time: 89.3 us; the launch traced here: 88.9 us
  Pallas kernels  82.6 us (92%)
  local copies, waits for them, and re-layouts  6.26 us (7%)
    pallas_call x1, Pallas kernels, body(): pl.pallas_call(kernel, name='tree_step', out_shape=jax.ShapeDtypeStruct((...  82.6 us
    unnamed x15, local copies, waits for them, and re-layouts  6.26 us

profile of v1, /device:TPU:1, one launch (start us, length us, event | category | flops | bytes accessed | tf_op | source)
XLA Modules:
  0.0 88.9 jit_solution(11044419324560541066)
XLA Ops:
  0.0 0.0 copy-start
  0.0 1.0 %copy-done = bf16[256,640]{1,0:T(8,128)(2,1)S(1)} copy-done((bf16[256,640]{1,0:T(8,128)(2,1)S(1)}, bf16[256,640]{1,0:T(8,128)(2,1)}, u32[]{:S(2)}) %copy-start) | copy-done | bytes 327704
  1.0 0.0 copy-start.1
  1.0 0.8 copy-done.1
  1.8 0.0 copy-start.2
  1.8 0.8 copy-done.2
  2.7 0.0 copy-start.3
  2.7 0.8 copy-done.3
  3.4 0.0 copy-start.4
  3.4 0.7 copy-done.4
  4.1 0.0 copy-start.5
  4.1 0.7 copy-done.5
  4.8 0.0 copy-start.6
  4.8 0.7 copy-done.6
  5.5 82.6 %tree_step.1 = bf16[32,5120]{1,0:T(8,128)(2,1)S(1)} custom-call(bf16[256,640]{1,0:T(8,128)(2,1)S(1)} %copy-done, bf16[256,128]{1,0:T(8,128)(2,1)S(1)} %copy-done.1, bf16[256,128]{1,0:T(8,128)(2,1)S(1)} %copy-done.2, bf16[64,128]{1,0:T(8,128)(2,1)S(1)} %copy-done.4, bf16[64,128]{1,0:T(8,128)(2,1)S(1)} %copy-done.5, s32[64,64]{1,0:T(8,128)S(1)} %copy-done.3, ...), custom_call_target="tpu_custom_call" | custom-call | tf_op jit(solution)/shard_map/tree_step/pallas_call | solution.py:231
  88.2 0.7 copy.9
Async XLA Ops:
  0.0 1.0 %copy-start = (bf16[256,640]{1,0:T(8,128)(2,1)S(1)}, bf16[256,640]{1,0:T(8,128)(2,1)}, u32[]{:S(2)}) copy-start(bf16[256,640]{1,0:T(8,128)(2,1)} %q.1) | copy-start | bytes 983044
  1.0 0.8 copy-start.1
  1.8 0.8 copy-start.2
  2.7 0.8 copy-start.3
  3.4 0.7 copy-start.4
  4.1 0.7 copy-start.5
  4.8 0.7 copy-start.6

commit v2 on v1

--- a/solution.py
+++ b/solution.py
@@ -43,12 +43,15 @@
     return jnp.where(mask, 1.0, 0.0).astype(BF)
 
 
-def kernel(q, bk, bv, sk, sv, anc, plan, out, kbuf, vbuf, kcat, vcat, pack, pick, *rest):
+def kernel(
+    q_in, bk_in, bv_in, sk, sv, anc_in, plan_in, out,
+    q, anc, plan, kbuf, vbuf, kcat, vcat, pack, pack_row, by_row, pick, *rest
+):
     snd, rest = rest[:N_CH], rest[N_CH:]
     rcv, rest = rest[:N_CH], rest[N_CH:]
     tsnd, rest = rest[:N_CH], rest[N_CH:]
     trcv, rest = rest[:N_CH], rest[N_CH:]
-    send_k, send_v, got_ka, got_va, got_kb, got_vc, got_kc, got_vb, a_send, a_got, t_send, t_got = rest
+    send_k, send_v, got_ka, got_va, got_kb, got_vc, got_kc, got_vb, a_send, a_got, t_send, t_got, load = rest
 
     dp = lax.axis_index("dp")
     t = lax.axis_index("tensor")
@@ -61,6 +64,18 @@
     far = [at(4 * i, 0) for i in (2, 1, 3)]
     near = [at(d, 0) for d in (1, -1, 2, -2)]
     side = [at(0, i) for i in (1, 2, 3)]
+
+    k_own = x * 16 + zm * 4 + zd
+    v_own = zm * 16 + x * 4 + zd
+    loads = [
+        pltpu.make_async_copy(src, dst, load.at[i])
+        for i, (src, dst) in enumerate((
+            (sk, kbuf.at[k_own]), (sv, vbuf.at[v_own]), (anc_in, anc), (plan_in, plan),
+            (q_in, q), (bk_in, kcat.at[pl.ds(0, STEP)]), (bv_in, vcat.at[pl.ds(0, STEP)]),
+        ))
+    ]
+    for copy in loads:
+        copy.start()
 
     barrier = pltpu.get_barrier_semaphore()
     for peer in far + near + side:
@@ -81,14 +96,15 @@
         view = buf.at[pl.ds(0, count)]
         pltpu.make_async_copy(view, view, sem).wait()
 
-    k_own = x * 16 + zm * 4 + zd
-    v_own = zm * 16 + x * 4 + zd
+    loads[0].wait()
     for peer in far:
-        put(sk, kbuf.at[k_own], send_k, got_ka, peer)
+        put(kbuf.at[k_own], kbuf.at[k_own], send_k, got_ka, peer)
+    loads[1].wait()
     for peer in far:
-        put(sv, vbuf.at[v_own], send_v, got_va, peer)
-    kbuf[k_own] = sk[...]
-    vbuf[v_own] = sv[...]
+        put(vbuf.at[v_own], vbuf.at[v_own], send_v, got_va, peer)
+
+    for copy in loads[2:]:
+        copy.wait()
 
     def scan(s, carry):
         count, ids = carry
@@ -111,9 +127,15 @@
     mine = jnp.sum(jnp.where(iota((N_DP, STEP), 0) == dp, dest, 0.0), axis=0, keepdims=True)
     row_code = mine.astype(jnp.int32) * UNIT + (iota((1, STEP), 1) & 7)
     pack[...] = flag(iota((N_DP * UNIT, STEP), 0) == row_code)
+    unit_of = flag((iota((UNITS_DEV, STEP), 1) & 31) == iota((UNITS_DEV, STEP), 0))
+    dest = dot(table.astype(BF), unit_of)
+    mine = jnp.sum(jnp.where(iota((N_DP, STEP), 0) == dp, dest, 0.0), axis=0, keepdims=True)
+    row_code = mine.astype(jnp.int32) * N_T + (iota((1, STEP), 1) >> 5)
+    pack_row[...] = flag(iota((N_DP * N_T, STEP), 0) == row_code)
+    row, col = iota((STEP, STEP), 0), iota((STEP, STEP), 1)
+    by_row[...] = flag((row & 31) * UNIT + (row >> 5) == col)
     to_me = flag(table == dp.astype(F32))
-    by_row = flag((iota((STEP, UNITS_DEV), 0) & 31) == iota((STEP, UNITS_DEV), 1))
-    source = dot(by_row, to_me, ((1,), (1,)))
+    source = dot(unit_of, to_me, ((0,), (1,)))
     widen_dp = flag((iota((N_DP, N_DP * UNIT), 1) >> 3) == iota((N_DP, N_DP * UNIT), 0))
     source = dot(source.astype(BF), widen_dp)
     same_row = (iota((STEP, N_DP * UNIT), 0) >> 5) == (iota((STEP, N_DP * UNIT), 1) & 7)
@@ -141,8 +163,6 @@
         put(vbuf.at[pl.ds(v_start, 4)], vbuf.at[pl.ds(v_start, 4)], send_v, got_vc.at[i], side[i])
     k_across(zm)
     to_near(vbuf, v_start, send_v, [got_vb] * 3)
-    kcat[pl.ds(0, STEP), :] = bk[...]
-    vcat[pl.ds(0, STEP), :] = bv[...]
     for i, shift in enumerate((3, 1, 2)):
         await_blocks(kbuf, 4, got_kb.at[i])
         k_across(lax.rem(zm + shift, 4))
@@ -165,28 +185,24 @@
     bias = jnp.where(col < STEP + count * BLOCK, 0.0, FILL)
     causal = iota((STEP, STEP), 1) <= iota((STEP, STEP), 0)
 
-    head = 0
-    for c, heads in enumerate(CHUNKS):
-        for h in range(heads):
-            qh = q[:, pl.ds(head * HEAD_DIM, HEAD_DIM)]
-            head += 1
-            scores = dot(qh, kcat[...], ((1,), (1,)))
-            local = jnp.where(causal, scores[:, :STEP], FILL)
-            shared = scores[:, STEP:] + bias[:, STEP:]
-            top = jnp.maximum(
-                jnp.max(local, axis=1, keepdims=True), jnp.max(shared, axis=1, keepdims=True)
-            )
-            local = jnp.exp2((local - top) * SCALE)
-            shared = jnp.exp2((shared - top) * SCALE)
-            total = jnp.sum(local, axis=1, keepdims=True) + jnp.sum(shared, axis=1, keepdims=True)
-            acc = dot(local.astype(BF), vcat[pl.ds(0, STEP), :]) + dot(
-                shared.astype(BF), vcat[pl.ds(STEP, MOST * BLOCK), :]
-            )
-            merged = (acc / total).astype(BF)
-            slots = dot(pack[...], merged).astype(BF)
-            snd[c][:, :, pl.ds(h * HEAD_DIM, HEAD_DIM)] = slots.reshape(N_DP, UNIT, HEAD_DIM)
-
-        def send_one(i, carry, c=c):
+    def attend(head):
+        qh = q[:, pl.ds(head * HEAD_DIM, HEAD_DIM)]
+        scores = dot(qh, kcat[...], ((1,), (1,)))
+        local = jnp.where(causal, scores[:, :STEP], FILL)
+        shared = scores[:, STEP:] + bias[:, STEP:]
+        top = jnp.maximum(
+            jnp.max(local, axis=1, keepdims=True), jnp.max(shared, axis=1, keepdims=True)
+        )
+        local = jnp.exp2((local - top) * SCALE)
+        shared = jnp.exp2((shared - top) * SCALE)
+        total = jnp.sum(local, axis=1, keepdims=True) + jnp.sum(shared, axis=1, keepdims=True)
+        acc = dot(local.astype(BF), vcat[pl.ds(0, STEP), :]) + dot(
+            shared.astype(BF), vcat[pl.ds(STEP, MOST * BLOCK), :]
+        )
+        return (acc / total).astype(BF)
+
+    def send_dp(c):
+        def send_one(i, carry):
             peer = lax.rem(dp + i, N_DP)
             put(snd[c].at[peer], rcv[c].at[dp], a_send.at[c], a_got.at[c], peer)
             return carry
@@ -194,11 +210,7 @@
         lax.fori_loop(1, N_DP, send_one, 0)
         rcv[c][dp] = snd[c][dp]
 
-    for c, heads in enumerate(CHUNKS):
-        await_blocks(rcv[c], N_DP - 1, a_got.at[c])
-        wide = heads * HEAD_DIM
-        rows = dot(pick[...], rcv[c][...].reshape(N_DP * UNIT, wide)).astype(BF)
-        tsnd[c][...] = rows.reshape(N_T, UNITS_DEV, wide)
+    def send_tensor(c):
         for i in range(1, N_T):
             peer = lax.rem(t + i, N_T)
             pltpu.make_async_remote_copy(
@@ -208,12 +220,47 @@
             ).start()
         trcv[c][t] = tsnd[c][t]
 
+    def picked(c):
+        await_blocks(rcv[c], N_DP - 1, a_got.at[c])
+        slots = rcv[c][...].reshape(N_DP * UNIT, CHUNKS[c] * HEAD_DIM)
+        return dot(pick[...], slots).astype(BF)
+
+    last = N_CH - 1
+    head = 0
+    for c, heads in enumerate(CHUNKS):
+        for h in range(heads):
+            merged = attend(head)
+            head += 1
+            place = pl.ds(h * HEAD_DIM, HEAD_DIM)
+            if c < last:
+                slots = dot(pack[...], merged).astype(BF)
+                snd[c][:, :, place] = slots.reshape(N_DP, UNIT, HEAD_DIM)
+            else:
+                rows = dot(by_row[...], merged).astype(BF)
+                tsnd[c][:, :, place] = rows.reshape(N_T, UNITS_DEV, HEAD_DIM)
+        if c < last:
+            send_dp(c)
+        else:
+            send_tensor(c)
+    await_blocks(trcv[last], N_T - 1, t_got.at[last])
+    wide = CHUNKS[last] * HEAD_DIM
+    slots = dot(pack_row[...], trcv[last][...].reshape(STEP, wide)).astype(BF)
+    snd[last][...] = slots.reshape(N_DP, N_T, wide)
+    send_dp(last)
+
+    for c in range(last):
+        tsnd[c][...] = picked(c).reshape(N_T, UNITS_DEV, CHUNKS[c] * HEAD_DIM)
+        send_tensor(c)
     start = 0
     for c, heads in enumerate(CHUNKS):
-        await_blocks(trcv[c], N_T - 1, t_got.at[c])
         wide = heads * HEAD_DIM
+        if c < last:
+            await_blocks(trcv[c], N_T - 1, t_got.at[c])
+        else:
+            rows = picked(c)
         for peer in range(N_T):
-            out[:, pl.ds(peer * PER * HEAD_DIM + start, wide)] = trcv[c][peer]
+            part = trcv[c][peer] if c < last else rows[peer * UNITS_DEV : (peer + 1) * UNITS_DEV]
+            out[:, pl.ds(peer * PER * HEAD_DIM + start, wide)] = part
         start += wide
 
     await_blocks(kbuf, 63, send_k)
@@ -225,35 +272,45 @@
 
 def body(queries, branch_keys, branch_values, shared_keys, shared_values, ancestry, plan):
     vmem = pl.BlockSpec(memory_space=pltpu.VMEM)
-    smem = pl.BlockSpec(memory_space=pltpu.SMEM)
+    hbm = pl.BlockSpec(memory_space=pltpu.HBM)
     widths = [heads * HEAD_DIM for heads in CHUNKS]
     dma = pltpu.SemaphoreType.DMA
     rows = pl.pallas_call(
         kernel,
         name="tree_step",
-        out_shape=jax.ShapeDtypeStruct((UNITS_DEV, HEADS * HEAD_DIM), BF),
-        in_specs=[vmem] * 5 + [smem, vmem],
+        out_shape=pltpu.VMEM((UNITS_DEV, HEADS * HEAD_DIM), BF),
+        in_specs=[hbm] * 7,
         out_specs=vmem,
         scratch_shapes=[
+            pltpu.VMEM((STEP, PER * HEAD_DIM), BF),
+            pltpu.SMEM((N_DP, SHARED), jnp.int32),
+            pltpu.VMEM((16, 128), jnp.int32),
             pltpu.VMEM((SHARED, BLOCK, HEAD_DIM), BF),
             pltpu.VMEM((SHARED, BLOCK, HEAD_DIM), BF),
             pltpu.VMEM((KEYS, HEAD_DIM), BF),
             pltpu.VMEM((KEYS, HEAD_DIM), BF),
             pltpu.VMEM((N_DP * UNIT, STEP), BF),
+            pltpu.VMEM((N_DP * N_T, STEP), BF),
+            pltpu.VMEM((STEP, STEP), BF),
             pltpu.VMEM((STEP, N_DP * UNIT), BF),
             *[pltpu.VMEM((N_DP, UNIT, w), BF) for w in widths],
             *[pltpu.VMEM((N_DP, UNIT, w), BF) for w in widths],
             *[pltpu.VMEM((N_T, UNITS_DEV, w), BF) for w in widths],
             *[pltpu.VMEM((N_T, UNITS_DEV, w), BF) for w in widths],
             dma, dma, dma, dma, dma((3,)), dma((3,)), dma, dma,
-            dma((N_CH,)), dma((N_CH,)), dma((N_CH,)), dma((N_CH,)),
+            dma((N_CH,)), dma((N_CH,)), dma((N_CH,)), dma((N_CH,)), dma((7,)),
         ],
         compiler_params=pltpu.CompilerParams(
             collective_id=0, has_side_effects=True, vmem_limit_bytes=40 << 20
         ),
     )(
-        queries, branch_keys, branch_values, shared_keys, shared_values, ancestry,
-        plan.reshape(16, 128),
+        *[
+            pltpu.with_memory_space_constraint(a, pltpu.HBM)
+            for a in (
+                queries, branch_keys, branch_values, shared_keys, shared_values, ancestry,
+                plan.reshape(16, 128),
+            )
+        ]
     )
     return rows.reshape(UNITS_DEV, 1, HEADS * HEAD_DIM)
 

time: 89.3 us -> 76.2 us (0.85)
  the two profiles are of different devices: /device:TPU:1 before, /device:TPU:16 now
where the time goes in v2:
time: 76.2 us; the launch traced here: 76.1 us
  Pallas kernels  75.4 us (99%)
    pallas_call x1, Pallas kernels, body(): pl.pallas_call(kernel, name='tree_step', out_shape=pltpu.VMEM((UNITS_DEV,...  75.4 us

profile of v2, /device:TPU:16, one launch (start us, length us, event | category | flops | bytes accessed | tf_op | source)
XLA Modules:
  0.0 76.1 jit_solution(14387275146521576530)
XLA Ops:
  0.0 75.4 %tree_step.1 = bf16[32,5120]{1,0:T(8,128)(2,1)S(1)} custom-call(bf16[256,640]{1,0:T(8,128)(2,1)} %q_in.1, bf16[256,128]{1,0:T(8,128)(2,1)} %bk_in.1, bf16[256,128]{1,0:T(8,128)(2,1)} %bv_in.1, bf16[64,128]{1,0:T(8,128)(2,1)} %sk.1, bf16[64,128]{1,0:T(8,128)(2,1)} %sv.1, s32[64,64]{1,0:T(8,128)} %anc_in.1, s32[16,128]{1,0:T(8,128)} %bitcast.3), custom_call_target="tpu_custom_call" | custom-call | tf_op jit(solution)/shard_map/tree_step/pallas_call | solution.py:278
  75.4 0.7 copy.9

commit v3 on v2

--- a/solution.py
+++ b/solution.py
@@ -21,7 +21,7 @@
 N_Z = 16
 N_T = 8
 PER = HEADS // KV_HEADS
-CHUNKS = (1, 2, 2)
+CHUNKS = (2, 3)
 N_CH = len(CHUNKS)
 KEYS = STEP + MOST * BLOCK
 SCALE = math.log2(math.e) / math.sqrt(HEAD_DIM)
@@ -55,11 +55,11 @@
 
     dp = lax.axis_index("dp")
     t = lax.axis_index("tensor")
-    z, x = lax.div(dp, N_X), lax.rem(dp, N_X)
-    zm, zd = lax.rem(z, 4), lax.div(z, 4)
+    z, x = dp >> 2, dp & 3
+    zm, zd = z & 3, z >> 2
 
     def at(dz, dx):
-        return lax.rem(z + (dz + N_Z), N_Z) * N_X + lax.rem(x + dx, N_X)
+        return (((z + dz) & (N_Z - 1)) << 2) + ((x + dx) & (N_X - 1))
 
     far = [at(4 * i, 0) for i in (2, 1, 3)]
     near = [at(d, 0) for d in (1, -1, 2, -2)]
@@ -74,22 +74,24 @@
             (q_in, q), (bk_in, kcat.at[pl.ds(0, STEP)]), (bv_in, vcat.at[pl.ds(0, STEP)]),
         ))
     ]
-    for copy in loads:
+    for copy in loads[:2]:
         copy.start()
 
     barrier = pltpu.get_barrier_semaphore()
     for peer in far + near + side:
-        pl.semaphore_signal(barrier, inc=1, device_id={"dp": peer}, device_id_type=MESH)
+        pl.semaphore_signal(barrier, inc=1, device_id=(peer, t), device_id_type=MESH)
     for i in range(1, N_T):
         pl.semaphore_signal(
-            barrier, inc=1, device_id={"tensor": lax.rem(t + i, N_T)}, device_id_type=MESH
+            barrier, inc=1, device_id=(dp, (t + i) & (N_T - 1)), device_id_type=MESH
         )
+    for copy in loads[2:]:
+        copy.start()
     pl.semaphore_wait(barrier, len(far) + len(near) + len(side) + N_T - 1)
 
     def put(src, dst, send, got, peer):
         pltpu.make_async_remote_copy(
             src_ref=src, dst_ref=dst, send_sem=send, recv_sem=got,
-            device_id={"dp": peer}, device_id_type=MESH,
+            device_id=(peer, t), device_id_type=MESH,
         ).start()
 
     def await_blocks(buf, count, sem):
@@ -148,10 +150,13 @@
         for peer in side:
             put(k_group(g), k_group(g), send_k, got_kc, peer)
 
-    def to_near(buf, start, send, gots):
+    def to_near(buf, start, send, gots, way=None):
         whole = buf.at[pl.ds(start, 4)]
         put(whole, whole, send, gots[0], near[0])
         put(whole, whole, send, gots[1], near[1])
+        if way is not None:
+            put(whole, whole, send, gots[2], near[2 + way])
+            return
         put(buf.at[pl.ds(start, 2)], buf.at[pl.ds(start, 2)], send, gots[2], near[2])
         put(buf.at[pl.ds(start + 2, 2)], buf.at[pl.ds(start + 2, 2)], send, gots[2], near[3])
 
@@ -162,13 +167,13 @@
     for i in range(3):
         put(vbuf.at[pl.ds(v_start, 4)], vbuf.at[pl.ds(v_start, 4)], send_v, got_vc.at[i], side[i])
     k_across(zm)
-    to_near(vbuf, v_start, send_v, [got_vb] * 3)
+    to_near(vbuf, v_start, send_v, [got_vb] * 3, 0)
     for i, shift in enumerate((3, 1, 2)):
         await_blocks(kbuf, 4, got_kb.at[i])
-        k_across(lax.rem(zm + shift, 4))
+        k_across((zm + shift) & 3)
     for i in range(3):
         await_blocks(vbuf, 4, got_vc.at[i])
-        to_near(vbuf, zm * 16 + lax.rem(x + 3 - i, 4) * 4, send_v, [got_vb] * 3)
+        to_near(vbuf, zm * 16 + ((x + 3 - i) & 3) * 4, send_v, [got_vb] * 3, (i + 1) & 1)
 
     await_blocks(kbuf, 48, got_kc)
     for k in range(MOST):
@@ -203,20 +208,27 @@
 
     def send_dp(c):
         def send_one(i, carry):
-            peer = lax.rem(dp + i, N_DP)
-            put(snd[c].at[peer], rcv[c].at[dp], a_send.at[c], a_got.at[c], peer)
+            m = i >> 2
+            half = (m + 1) >> 1
+            pz = jnp.where((m & 1) == 1, half, (N_Z - half) & (N_Z - 1))
+            peer = (pz << 2) + ((i + x) & (N_X - 1))
+
+            @pl.when(peer != dp)
+            def _():
+                put(snd[c].at[peer], rcv[c].at[dp], a_send.at[c], a_got.at[c], peer)
+
             return carry
 
-        lax.fori_loop(1, N_DP, send_one, 0)
+        lax.fori_loop(0, N_DP, send_one, 0)
         rcv[c][dp] = snd[c][dp]
 
     def send_tensor(c):
         for i in range(1, N_T):
-            peer = lax.rem(t + i, N_T)
+            peer = (t + i) & (N_T - 1)
             pltpu.make_async_remote_copy(
                 src_ref=tsnd[c].at[peer], dst_ref=trcv[c].at[t],
                 send_sem=t_send.at[c], recv_sem=t_got.at[c],
-                device_id={"tensor": peer}, device_id_type=MESH,
+                device_id=(dp, peer), device_id_type=MESH,
             ).start()
         trcv[c][t] = tsnd[c][t]
 

time: 76.2 us -> 72.2 us (0.948)
  the two profiles are of different devices: /device:TPU:16 before, /device:TPU:128 now
where the time goes in v3:
time: 72.2 us; the launch traced here: 71.8 us
  Pallas kernels  71.1 us (98%)
  local copies, waits for them, and re-layouts  0.73 us (1%)
    pallas_call x1, Pallas kernels, body(): pl.pallas_call(kernel, name='tree_step', out_shape=pltpu.VMEM((UNITS_DEV,...  71.1 us

profile of v3, /device:TPU:128, one launch (start us, length us, event | category | flops | bytes accessed | tf_op | source)
XLA Modules:
  0.0 71.8 jit_solution(9500856531269917878)
XLA Ops:
  0.0 71.1 %tree_step.1 = bf16[32,5120]{1,0:T(8,128)(2,1)S(1)} custom-call(bf16[256,640]{1,0:T(8,128)(2,1)} %q_in.1, bf16[256,128]{1,0:T(8,128)(2,1)} %bk_in.1, bf16[256,128]{1,0:T(8,128)(2,1)} %bv_in.1, bf16[64,128]{1,0:T(8,128)(2,1)} %sk.1, bf16[64,128]{1,0:T(8,128)(2,1)} %sv.1, s32[64,64]{1,0:T(8,128)} %anc_in.1, s32[16,128]{1,0:T(8,128)} %bitcast.3), custom_call_target="tpu_custom_call" | custom-call | tf_op jit(solution)/shard_map/tree_step/pallas_call | solution.py:290
  71.1 0.7 %copy.9 = bf16[32,1,5120]{2,0,1:T(8,128)(2,1)} copy(bf16[32,1,5120]{2,0,1:T(8,128)(2,1)S(1)} %bitcast.2) | data formatting | bytes 655360

commit v4 on v3

--- a/solution.py
+++ b/solution.py
@@ -56,17 +56,21 @@
     dp = lax.axis_index("dp")
     t = lax.axis_index("tensor")
     z, x = dp >> 2, dp & 3
-    zm, zd = z & 3, z >> 2
 
     def at(dz, dx):
         return (((z + dz) & (N_Z - 1)) << 2) + ((x + dx) & (N_X - 1))
 
-    far = [at(4 * i, 0) for i in (2, 1, 3)]
+    far = [at(4 * i, 0) for i in (1, 2, 3)]
     near = [at(d, 0) for d in (1, -1, 2, -2)]
     side = [at(0, i) for i in (1, 2, 3)]
 
-    k_own = x * 16 + zm * 4 + zd
-    v_own = zm * 16 + x * 4 + zd
+    def k_at(c, i, count):
+        return kbuf.at[pl.ds(x * 16 + c * 4 + i, count)]
+
+    def v_at(c, bx, i, count):
+        return vbuf.at[pl.ds(c * 16 + bx * 4 + i, count)]
+
+    k_own, v_own = x * 16, x * 4
     loads = [
         pltpu.make_async_copy(src, dst, load.at[i])
         for i, (src, dst) in enumerate((
@@ -98,12 +102,33 @@
         view = buf.at[pl.ds(0, count)]
         pltpu.make_async_copy(view, view, sem).wait()
 
+    def k_side(c, i, count):
+        for peer in side:
+            put(k_at(c, i, count), k_at(c, i, count), send_k, got_kc, peer)
+
+    def v_side(i, count, got):
+        for n, peer in enumerate(side):
+            put(v_at(0, x, i, count), v_at(0, x, i, count), send_v, got.at[n], peer)
+
+    def v_near(bx, i, count):
+        block = v_at(0, bx, i, count)
+        put(block, v_at(1, bx, i, count), send_v, got_vb, near[0])
+        put(block, v_at(2, bx, i, count), send_v, got_vb, near[1])
+        third = jnp.where((bx & 1) == 1, near[3], near[2])
+        put(block, v_at(3, bx, i, count), send_v, got_vb, third)
+
+    order = (1, 0, 2)
     loads[0].wait()
-    for peer in far:
-        put(kbuf.at[k_own], kbuf.at[k_own], send_k, got_ka, peer)
+    for n in order:
+        put(kbuf.at[k_own], kbuf.at[k_own + 3 - n], send_k, got_ka, far[n])
     loads[1].wait()
-    for peer in far:
-        put(vbuf.at[v_own], vbuf.at[v_own], send_v, got_va, peer)
+    for n in order:
+        put(vbuf.at[v_own], vbuf.at[v_own + 3 - n], send_v, got_va, far[n])
+    for n in (0, 1, 2):
+        put(k_at(0, 0, 1), k_at(n + 1, 0, 1), send_k, got_kb.at[0, n], near[n])
+    v_side(0, 1, got_vc.at[0])
+    k_side(0, 0, 1)
+    v_near(x, 0, 1)
 
     for copy in loads[2:]:
         copy.wait()
@@ -143,48 +168,42 @@
     same_row = (iota((STEP, N_DP * UNIT), 0) >> 5) == (iota((STEP, N_DP * UNIT), 1) & 7)
     pick[...] = jnp.where(same_row, source, 0.0).astype(BF)
 
-    def k_group(g):
-        return kbuf.at[pl.ds(x * 16 + g * 4, 4)]
-
-    def k_across(g):
-        for peer in side:
-            put(k_group(g), k_group(g), send_k, got_kc, peer)
-
-    def to_near(buf, start, send, gots, way=None):
-        whole = buf.at[pl.ds(start, 4)]
-        put(whole, whole, send, gots[0], near[0])
-        put(whole, whole, send, gots[1], near[1])
-        if way is not None:
-            put(whole, whole, send, gots[2], near[2 + way])
-            return
-        put(buf.at[pl.ds(start, 2)], buf.at[pl.ds(start, 2)], send, gots[2], near[2])
-        put(buf.at[pl.ds(start + 2, 2)], buf.at[pl.ds(start + 2, 2)], send, gots[2], near[3])
+    def forward(r, i, count):
+        for n in (0, 1, 2):
+            await_blocks(kbuf, count, got_kb.at[r, n])
+            k_side(n + 1, i, count)
+        for n in (0, 1, 2):
+            await_blocks(vbuf, count, got_vc.at[r, n])
+            v_near((x + 3 - n) & 3, i, count)
+
+    forward(0, 0, 1)
 
     await_blocks(kbuf, 3, got_ka)
-    to_near(kbuf, x * 16 + zm * 4, send_k, [got_kb.at[0], got_kb.at[1], got_kb.at[2]])
+    put(k_at(0, 1, 3), k_at(1, 1, 3), send_k, got_kb.at[1, 0], near[0])
+    put(k_at(0, 1, 3), k_at(2, 1, 3), send_k, got_kb.at[1, 1], near[1])
+    put(k_at(0, 1, 1), k_at(3, 1, 1), send_k, got_kb.at[1, 2], near[2])
+    put(k_at(0, 1, 2), k_at(3, 2, 2), send_k, got_kb.at[1, 2], near[3])
     await_blocks(vbuf, 3, got_va)
-    v_start = zm * 16 + x * 4
-    for i in range(3):
-        put(vbuf.at[pl.ds(v_start, 4)], vbuf.at[pl.ds(v_start, 4)], send_v, got_vc.at[i], side[i])
-    k_across(zm)
-    to_near(vbuf, v_start, send_v, [got_vb] * 3, 0)
-    for i, shift in enumerate((3, 1, 2)):
-        await_blocks(kbuf, 4, got_kb.at[i])
-        k_across((zm + shift) & 3)
-    for i in range(3):
-        await_blocks(vbuf, 4, got_vc.at[i])
-        to_near(vbuf, zm * 16 + ((x + 3 - i) & 3) * 4, send_v, [got_vb] * 3, (i + 1) & 1)
+    v_side(1, 3, got_vc.at[1])
+    k_side(0, 1, 3)
+    v_near(x, 1, 3)
+    forward(1, 1, 3)
+
+    def place(s, values):
+        bx, away = s & 3, ((s >> 2) - z) & (N_Z - 1)
+        low = away & 3
+        c = jnp.where(low == 0, 0, jnp.where(low == 1, 2, jnp.where(low == 2, 3, 1)))
+        two = jnp.where((bx & 1) == 1, 0, 2) if values else 2
+        more = jnp.where(low == 3, 1, jnp.where(low == 2, two, 0))
+        i = ((away + more) >> 2) & 3
+        return c * 16 + bx * 4 + i if values else bx * 16 + c * 4 + i
 
     await_blocks(kbuf, 48, got_kc)
     for k in range(MOST):
-        s = ids[k]
-        bx, bz = s & 3, s >> 2
-        kcat[pl.ds(STEP + k * BLOCK, BLOCK), :] = kbuf[bx * 16 + (bz & 3) * 4 + (bz >> 2)]
+        kcat[pl.ds(STEP + k * BLOCK, BLOCK), :] = kbuf[place(ids[k], False)]
     await_blocks(vbuf, 48, got_vb)
     for k in range(MOST):
-        s = ids[k]
-        bx, bz = s & 3, s >> 2
-        vcat[pl.ds(STEP + k * BLOCK, BLOCK), :] = vbuf[(bz & 3) * 16 + bx * 4 + (bz >> 2)]
+        vcat[pl.ds(STEP + k * BLOCK, BLOCK), :] = vbuf[place(ids[k], True)]
 
     col = iota((1, KEYS), 1)
     bias = jnp.where(col < STEP + count * BLOCK, 0.0, FILL)
@@ -309,7 +328,7 @@
             *[pltpu.VMEM((N_DP, UNIT, w), BF) for w in widths],
             *[pltpu.VMEM((N_T, UNITS_DEV, w), BF) for w in widths],
             *[pltpu.VMEM((N_T, UNITS_DEV, w), BF) for w in widths],
-            dma, dma, dma, dma, dma((3,)), dma((3,)), dma, dma,
+            dma, dma, dma, dma, dma((2, 3)), dma((2, 3)), dma, dma,
             dma((N_CH,)), dma((N_CH,)), dma((N_CH,)), dma((N_CH,)), dma((7,)),
         ],
         compiler_params=pltpu.CompilerParams(

time: 72.2 us -> 69.5 us (0.963)
  Pallas kernels: 71.1 us -> 68.7 us
    pallas_call x1, Pallas kernels: 71.1 us -> 68.7 us  [body(): pl.pallas_call(kernel, name='tree_step', out_shape=pltpu.VMEM((UNITS_DEV,...]
where the time goes in v4:
time: 69.5 us; the launch traced here: 69.4 us
  Pallas kernels  68.7 us (99%)
  local copies, waits for them, and re-layouts  0.73 us (1%)
    pallas_call x1, Pallas kernels, body(): pl.pallas_call(kernel, name='tree_step', out_shape=pltpu.VMEM((UNITS_DEV,...  68.7 us

profile of v4, /device:TPU:128, one launch (start us, length us, event | category | flops | bytes accessed | tf_op | source)
XLA Modules:
  0.0 69.4 jit_solution(2571516383309639570)
XLA Ops:
  0.0 68.7 %tree_step.1 = bf16[32,5120]{1,0:T(8,128)(2,1)S(1)} custom-call(bf16[256,640]{1,0:T(8,128)(2,1)} %q_in.1, bf16[256,128]{1,0:T(8,128)(2,1)} %bk_in.1, bf16[256,128]{1,0:T(8,128)(2,1)} %bv_in.1, bf16[64,128]{1,0:T(8,128)(2,1)} %sk.1, bf16[64,128]{1,0:T(8,128)(2,1)} %sv.1, s32[64,64]{1,0:T(8,128)} %anc_in.1, s32[16,128]{1,0:T(8,128)} %bitcast.3), custom_call_target="tpu_custom_call" | custom-call | tf_op jit(solution)/shard_map/tree_step/pallas_call | solution.py:309
  68.7 0.7 %copy.9 = bf16[32,1,5120]{2,0,1:T(8,128)(2,1)} copy(bf16[32,1,5120]{2,0,1:T(8,128)(2,1)S(1)} %bitcast.2) | data formatting | bytes 655360

commit v5 on v4

--- a/solution.py
+++ b/solution.py
@@ -45,7 +45,7 @@
 
 def kernel(
     q_in, bk_in, bv_in, sk, sv, anc_in, plan_in, out,
-    q, anc, plan, kbuf, vbuf, kcat, vcat, pack, pack_row, by_row, pick, *rest
+    q, anc, plan, kbuf, vbuf, kcat, vcat, weights, pack, pack_row, by_row, pick, *rest
 ):
     snd, rest = rest[:N_CH], rest[N_CH:]
     rcv, rest = rest[:N_CH], rest[N_CH:]
@@ -201,15 +201,11 @@
     await_blocks(kbuf, 48, got_kc)
     for k in range(MOST):
         kcat[pl.ds(STEP + k * BLOCK, BLOCK), :] = kbuf[place(ids[k], False)]
-    await_blocks(vbuf, 48, got_vb)
-    for k in range(MOST):
-        vcat[pl.ds(STEP + k * BLOCK, BLOCK), :] = vbuf[place(ids[k], True)]
-
     col = iota((1, KEYS), 1)
     bias = jnp.where(col < STEP + count * BLOCK, 0.0, FILL)
     causal = iota((STEP, STEP), 1) <= iota((STEP, STEP), 0)
 
-    def attend(head):
+    def weigh(head):
         qh = q[:, pl.ds(head * HEAD_DIM, HEAD_DIM)]
         scores = dot(qh, kcat[...], ((1,), (1,)))
         local = jnp.where(causal, scores[:, :STEP], FILL)
@@ -220,12 +216,29 @@
         local = jnp.exp2((local - top) * SCALE)
         shared = jnp.exp2((shared - top) * SCALE)
         total = jnp.sum(local, axis=1, keepdims=True) + jnp.sum(shared, axis=1, keepdims=True)
-        acc = dot(local.astype(BF), vcat[pl.ds(0, STEP), :]) + dot(
-            shared.astype(BF), vcat[pl.ds(STEP, MOST * BLOCK), :]
+        return local.astype(BF), shared.astype(BF), total
+
+    totals = []
+    for head in range(CHUNKS[0]):
+        local, shared, total = weigh(head)
+        weights[head, :, pl.ds(0, STEP)] = local
+        weights[head, :, pl.ds(STEP, MOST * BLOCK)] = shared
+        totals.append(total)
+
+    await_blocks(vbuf, 48, got_vb)
+    for k in range(MOST):
+        vcat[pl.ds(STEP + k * BLOCK, BLOCK), :] = vbuf[place(ids[k], True)]
+
+    def attend(head):
+        if head < CHUNKS[0]:
+            return (dot(weights[head], vcat[...]) / totals[head]).astype(BF)
+        local, shared, total = weigh(head)
+        acc = dot(local, vcat[pl.ds(0, STEP), :]) + dot(
+            shared, vcat[pl.ds(STEP, MOST * BLOCK), :]
         )
         return (acc / total).astype(BF)
 
-    def send_dp(c):
+    def send_dp(c, low, high):
         def send_one(i, carry):
             m = i >> 2
             half = (m + 1) >> 1
@@ -238,8 +251,7 @@
 
             return carry
 
-        lax.fori_loop(0, N_DP, send_one, 0)
-        rcv[c][dp] = snd[c][dp]
+        lax.fori_loop(low, high, send_one, 0)
 
     def send_tensor(c):
         for i in range(1, N_T):
@@ -270,14 +282,18 @@
                 rows = dot(by_row[...], merged).astype(BF)
                 tsnd[c][:, :, place] = rows.reshape(N_T, UNITS_DEV, HEAD_DIM)
         if c < last:
-            send_dp(c)
+            send_dp(c, 0, 32)
         else:
             send_tensor(c)
+            for before in range(last):
+                send_dp(before, 32, N_DP)
     await_blocks(trcv[last], N_T - 1, t_got.at[last])
     wide = CHUNKS[last] * HEAD_DIM
     slots = dot(pack_row[...], trcv[last][...].reshape(STEP, wide)).astype(BF)
     snd[last][...] = slots.reshape(N_DP, N_T, wide)
-    send_dp(last)
+    send_dp(last, 0, N_DP)
+    for c in range(N_CH):
+        rcv[c][dp] = snd[c][dp]
 
     for c in range(last):
         tsnd[c][...] = picked(c).reshape(N_T, UNITS_DEV, CHUNKS[c] * HEAD_DIM)
@@ -320,6 +336,7 @@
             pltpu.VMEM((SHARED, BLOCK, HEAD_DIM), BF),
             pltpu.VMEM((KEYS, HEAD_DIM), BF),
             pltpu.VMEM((KEYS, HEAD_DIM), BF),
+            pltpu.VMEM((CHUNKS[0], STEP, KEYS), BF),
             pltpu.VMEM((N_DP * UNIT, STEP), BF),
             pltpu.VMEM((N_DP * N_T, STEP), BF),
             pltpu.VMEM((STEP, STEP), BF),

time: 69.5 us -> 69 us (level)
  the two profiles are of different devices: /device:TPU:128 before, /device:TPU:96 now
where the time goes in v5:
time: 69 us; the launch traced here: 68.8 us
  Pallas kernels  68.1 us (99%)
  local copies, waits for them, and re-layouts  0.73 us (1%)
    pallas_call x1, Pallas kernels, body(): pl.pallas_call(kernel, name='tree_step', out_shape=pltpu.VMEM((UNITS_DEV,...  68.1 us

profile of v5, /device:TPU:96, one launch (start us, length us, event | category | flops | bytes accessed | tf_op | source)
XLA Modules:
  0.0 68.8 jit_solution(10399201267205260128)
XLA Ops:
  0.0 68.1 %tree_step.1 = bf16[32,5120]{1,0:T(8,128)(2,1)S(1)} custom-call(bf16[256,640]{1,0:T(8,128)(2,1)} %q_in.1, bf16[256,128]{1,0:T(8,128)(2,1)} %bk_in.1, bf16[256,128]{1,0:T(8,128)(2,1)} %bv_in.1, bf16[64,128]{1,0:T(8,128)(2,1)} %sk.1, bf16[64,128]{1,0:T(8,128)(2,1)} %sv.1, s32[64,64]{1,0:T(8,128)} %anc_in.1, s32[16,128]{1,0:T(8,128)} %bitcast.3), custom_call_target="tpu_custom_call" | custom-call | tf_op jit(solution)/shard_map/tree_step/pallas_call | solution.py:325
  68.1 0.7 %copy.9 = bf16[32,1,5120]{2,0,1:T(8,128)(2,1)} copy(bf16[32,1,5120]{2,0,1:T(8,128)(2,1)S(1)} %bitcast.2) | data formatting | bytes 655360

commit v6 on v5

--- a/solution.py
+++ b/solution.py
@@ -169,12 +169,11 @@
     pick[...] = jnp.where(same_row, source, 0.0).astype(BF)
 
     def forward(r, i, count):
-        for n in (0, 1, 2):
-            await_blocks(kbuf, count, got_kb.at[r, n])
-            k_side(n + 1, i, count)
-        for n in (0, 1, 2):
-            await_blocks(vbuf, count, got_vc.at[r, n])
-            v_near((x + 3 - n) & 3, i, count)
+        for k, v in ((0, 0), (1, 2), (2, 1)):
+            await_blocks(kbuf, count, got_kb.at[r, k])
+            k_side(k + 1, i, count)
+            await_blocks(vbuf, count, got_vc.at[r, v])
+            v_near((x + 3 - v) & 3, i, count)
 
     forward(0, 0, 1)
 
@@ -242,7 +241,8 @@
         def send_one(i, carry):
             m = i >> 2
             half = (m + 1) >> 1
-            pz = jnp.where((m & 1) == 1, half, (N_Z - half) & (N_Z - 1))
+            pz = jnp.where((m & 1) == 1, half + 1, N_Z + 1 - half)
+            pz = jnp.where(m < 3, m, pz)
             peer = (pz << 2) + ((i + x) & (N_X - 1))
 
             @pl.when(peer != dp)

time: 69 us -> 68.5 us (level)
  the two profiles are of different devices: /device:TPU:96 before, /device:TPU:128 now
where the time goes in v6:
time: 68.5 us; the launch traced here: 68.4 us
  Pallas kernels  67.6 us (99%)
  local copies, waits for them, and re-layouts  0.73 us (1%)
    pallas_call x1, Pallas kernels, body(): pl.pallas_call(kernel, name='tree_step', out_shape=pltpu.VMEM((UNITS_DEV,...  67.6 us

profile of v6, /device:TPU:128, one launch (start us, length us, event | category | flops | bytes accessed | tf_op | source)
XLA Modules:
  0.0 68.4 jit_solution(5589867084482868576)
XLA Ops:
  0.0 67.6 %tree_step.1 = bf16[32,5120]{1,0:T(8,128)(2,1)S(1)} custom-call(bf16[256,640]{1,0:T(8,128)(2,1)} %q_in.1, bf16[256,128]{1,0:T(8,128)(2,1)} %bk_in.1, bf16[256,128]{1,0:T(8,128)(2,1)} %bv_in.1, bf16[64,128]{1,0:T(8,128)(2,1)} %sk.1, bf16[64,128]{1,0:T(8,128)(2,1)} %sv.1, s32[64,64]{1,0:T(8,128)} %anc_in.1, s32[16,128]{1,0:T(8,128)} %bitcast.3), custom_call_target="tpu_custom_call" | custom-call | tf_op jit(solution)/shard_map/tree_step/pallas_call | solution.py:325
  67.7 0.7 %copy.9 = bf16[32,1,5120]{2,0,1:T(8,128)(2,1)} copy(bf16[32,1,5120]{2,0,1:T(8,128)(2,1)S(1)} %bitcast.2) | data formatting | bytes 655360
